TPU v7x, 512 devices: a whole 4x4x16 slice. The times are simulated.
512 devices in a mesh: leaf: 32 (over x, y, core), front: 16 (over z).
Axes of the slice: x: 4, y: 4, z: 16, core: 2. Of those that a mesh axis runs over, the one named last changes fastest.
Arguments:
- panel_0: float32 [2, 1024, 1024], P(None, 'front', 'leaf'), as said below
- panel_1: float32 [2, 1024, 2048], P(None, 'front', 'leaf'), as said below
- panel_2: float32 [2, 1024, 4096], P(None, 'front', 'leaf'), as said below
- panel_3: float32 [2, 1024, 8192], P(None, 'front', 'leaf'), as said below
- load_0: float32 [1024, 128], P('leaf'), may hold values from -6 to 6
- load_1: float32 [2048, 128], P('leaf'), may hold values from -6 to 6
- load_2: float32 [4096, 128], P('leaf'), may hold values from -6 to 6
- load_3: float32 [8192, 128], P('leaf'), may hold values from -6 to 6
- inflow: float32 [8, 1024, 128], P(None, 'front'), may hold values from -6 to 6
- above_solution: float32 [1024, 128], replicated, may hold values from -6 to 6
- block_maps: int32 [14, 16], replicated, may hold values from 0 to 31, as said below
Outputs:
- solution_0: float32 [1024, 128], P(('leaf', 'front'))
- solution_1: float32 [2048, 128], P(('leaf', 'front'))
- solution_2: float32 [4096, 128], P(('leaf', 'front'))
- solution_3: float32 [8192, 128], P(('leaf', 'front'))
- top_update: float32 [1024, 128], P('front')
Inputs may be any that keep to these rules, and one draw needn't show every extreme that they name: `block_maps`: the 16 entries of each row are distinct. `panel_0`: within each front the pivot block K is lower triangular with diagonal entries of 0.8 to 1.25. `panel_1`: within each front the pivot block K is lower triangular with diagonal entries of 0.8 to 1.25. `panel_2`: within each front the pivot block K is lower triangular with diagonal entries of 0.8 to 1.25. `panel_3`: within each front the pivot block K is lower triangular with diagonal entries of 0.8 to 1.25.
All inputs are finite; a program needn't handle non-finite values.
Results may differ from a plain program's by a relative error of at most 0.00013.
Values sent between devices are 32-bit elements; how exact they have to be, the bound alone decides.
No kernel may reach another device: no remote copies, remote signals or barrier semaphores. Data moves between devices by JAX's collectives and lax.ppermute only.
A program may use at most 64 MiB of HBM per device.

v0:
```python
import jax
import jax.numpy as jnp
from jax import lax
from jax.sharding import PartitionSpec as P

exact_precision = lax.Precision.HIGHEST


def partner_2(value, axis, distance):
    mask = 2**distance
    pairs = [(source, source ^ mask) for source in range(lax.axis_size(axis))]
    return lax.ppermute(value, axis, pairs)


def group_total(partial_sum, group_bits, level_id):
    leaf_pos = lax.axis_index("leaf")
    group_count = 1 << level_id
    slot_id = leaf_pos >> group_bits
    chosen = (jnp.arange(group_count, dtype=jnp.int32) == slot_id).astype(jnp.float32)
    spread_out = chosen.reshape((group_count,) + (1,) * partial_sum.ndim) * partial_sum[None]
    totals = lax.psum(spread_out, "leaf")
    return lax.dynamic_index_in_dim(totals, slot_id, 0, keepdims=False)


def group_concat(column_block, group_bits):
    leaf_pos = lax.axis_index("leaf")
    for section_bit in range(group_bits):
        partner = partner_2(column_block, "leaf", section_bit)
        upper_half = leaf_pos >> section_bit & 1 == 1
        column_block = jnp.where(
            upper_half,
            jnp.concatenate([partner, column_block], 0),
            jnp.concatenate([column_block, partner], 0),
        )
    return column_block


def place_blocks(map_row, values, block_rows):
    block_count = map_row.shape[0]
    targets = jnp.arange(2 * block_count, dtype=jnp.int32)
    selector_matrix = (targets[:, None] == map_row[None, :]).astype(jnp.float32)
    factor_blocks = values.reshape(block_count, block_rows, values.shape[1])
    return jnp.einsum("du,uye->dye", selector_matrix, factor_blocks, precision=exact_precision)


def lift_update(update_block, level_id, group_bits, block_maps, sep_rows):
    leaf_pos = lax.axis_index("leaf")
    front_pos = lax.axis_index("front")
    block_rows = update_block.shape[0]
    block_count = sep_rows // block_rows
    group_size = 1 << group_bits
    child_id = leaf_pos >> group_bits
    base_row = (1 << level_id) - 2
    own_map = lax.dynamic_index_in_dim(block_maps, base_row + child_id, 0, keepdims=False)
    parent_pos = leaf_pos % (2 * group_size)
    parent_rows = sep_rows // (2 * group_size)
    other_map = lax.dynamic_index_in_dim(block_maps, base_row + (child_id ^ 1), 0, keepdims=False)
    partner_block = partner_2(update_block, "leaf", group_bits)
    own_full, other_full = (
        lax.all_gather(update_block, "front", axis=0, tiled=True),
        lax.all_gather(partner_block, "front", axis=0, tiled=True),
    )
    placed = place_blocks(own_map, own_full, block_rows) + place_blocks(
        other_map, other_full, block_rows
    )
    separator = placed[:block_count].reshape(sep_rows, -1)
    sep_part = lax.dynamic_slice_in_dim(separator, parent_pos * parent_rows, parent_rows, 0)
    border = lax.dynamic_index_in_dim(placed, block_count + front_pos, 0, keepdims=False)
    return (sep_part, border)


def on_device(
    panel_0,
    panel_1,
    panel_2,
    panel_3,
    load_0,
    load_1,
    load_2,
    load_3,
    inflow,
    above_solution,
    block_maps,
):
    panels = (panel_0, panel_1, panel_2, panel_3)
    load_list = (load_0, load_1, load_2, load_3)
    level_count = len(panels)
    leaf_pos = lax.axis_index("leaf")
    front_pos = lax.axis_index("front")
    front_count = lax.axis_size("front")
    total_bits = lax.axis_size("leaf").bit_length() - 1
    block_rows = panel_0.shape[1]
    sep_rows = block_rows * front_count
    solved = [None] * level_count
    lifted = None
    top_block = None
    for level_id in range(level_count - 1, -1, -1):
        group_bits = total_bits - level_id
        right_side = load_list[level_id]
        if level_id == level_count - 1:
            front_id = leaf_pos >> group_bits
            border = lax.dynamic_index_in_dim(inflow, front_id, 0, keepdims=False)
        else:
            right_side = right_side + lifted[0]
            border = lifted[1]
        partial_sum = jnp.einsum(
            "ksc,cr->ksr", panels[level_id], right_side, precision=exact_precision
        )
        totals = group_total(partial_sum, group_bits, level_id)
        solved[level_id] = totals[0]
        update_block = border - totals[1]
        if level_id > 0:
            lifted = lift_update(update_block, level_id, group_bits, block_maps, sep_rows)
        else:
            top_block = update_block
    upper_full = above_solution
    upper_block = lax.dynamic_slice_in_dim(above_solution, front_pos * block_rows, block_rows, 0)
    targets = jnp.arange(2 * front_count, dtype=jnp.int32)
    pieces = []
    for level_id in range(level_count):
        group_bits = total_bits - level_id
        stacked = jnp.stack([solved[level_id], -upper_block])
        partial_sum = jnp.einsum(
            "ksc,ksr->cr", panels[level_id], stacked, precision=exact_precision
        )
        column_block = lax.psum(partial_sum, "front")
        span_rows = column_block.shape[0] // front_count
        pieces.append(lax.dynamic_slice_in_dim(column_block, front_pos * span_rows, span_rows, 0))
        if level_id < level_count - 1:
            full_solution = group_concat(column_block, group_bits)
            ancestor_blocks = jnp.concatenate([full_solution, upper_full], 0).reshape(
                2 * front_count, block_rows, -1
            )
            child_id = leaf_pos >> group_bits - 1
            child_map = lax.dynamic_index_in_dim(
                block_maps, (2 << level_id) - 2 + child_id, 0, keepdims=False
            )
            selector_matrix = (child_map[:, None] == targets[None, :]).astype(jnp.float32)
            upper_factor_blocks = jnp.einsum(
                "gq,qzk->gzk", selector_matrix, ancestor_blocks, precision=exact_precision
            )
            upper_full = upper_factor_blocks.reshape(sep_rows, -1)
            upper_block = lax.dynamic_index_in_dim(
                upper_factor_blocks, front_pos, 0, keepdims=False
            )
    return (pieces[0], pieces[1], pieces[2], pieces[3], top_block)


def solution(mesh):
    in_specs = (
        P(None, "front", "leaf"),
        P(None, "front", "leaf"),
        P(None, "front", "leaf"),
        P(None, "front", "leaf"),
        P("leaf", None),
        P("leaf", None),
        P("leaf", None),
        P("leaf", None),
        P(None, "front", None),
        P(),
        P(),
    )
    out_specs = (
        P(("leaf", "front"), None),
        P(("leaf", "front"), None),
        P(("leaf", "front"), None),
        P(("leaf", "front"), None),
        P("front", None),
    )
    return jax.shard_map(
        on_device, mesh=mesh, in_specs=in_specs, out_specs=out_specs, check_vma=False
    )
```

profile of v0, /device:TPU:2, one launch (start us, length us, event | category | flops | bytes accessed | tf_op | source)
XLA Modules:
  0.0 1208.8 jit_solution(1407500976551751530)
XLA Ops:
  8.1 1.2 fusion.16
  11.1 138.3 %all-reduce.7.cloned.1.call-done = f32[8,2,64,128]{3,2,1,0:T(8,128)} async-done(((f32[8,2,64,128]{3,2,1,0:T(8,128)}), f32[8,2,64,128]{3,2,1,0:T(8,128)}) %all-reduce.7.cloned.1.call-update) | async-done | bytes 524304 | tf_op jit(solution)/shard_map/psum | solution.py:21
  150.2 4.2 collective-permute-start
  154.4 33.1 %all_gather.18 = f32[1024,128]{1,0:T(8,128)S(1)} all-gather(f32[64,128]{1,0:T(8,128)S(1)} %fusion.32), channel_id=1, replica_groups=mesh['leaf'=32,'front'=16] {'front'}, dimensions={0}, use_global_device_ids=true | all-gather | bytes 557056 | tf_op jit(solution)/shard_map/all_gather | solution.py:60
  188.5 30.6 %all_gather.19 = f32[1024,128]{1,0:T(8,128)S(1)} all-gather(f32[64,128]{1,0:T(8,128)S(1)} %collective-permute-done), channel_id=1, replica_groups=mesh['leaf'=32,'front'=16] {'front'}, dimensions={0}, use_global_device_ids=true | all-gather | bytes 557056 | tf_op jit(solution)/shard_map/all_gather | solution.py:61
  219.1 1.0 convolution_add_fusion.2
  222.2 127.9 %all-reduce.9.cloned.1.call-done = f32[4,2,64,128]{3,2,1,0:T(8,128)} async-done(((f32[4,2,64,128]{3,2,1,0:T(8,128)}), f32[4,2,64,128]{3,2,1,0:T(8,128)}) %all-reduce.9.cloned.1.call-update) | async-done | bytes 262160 | tf_op jit(solution)/shard_map/psum | solution.py:21
  350.8 3.0 collective-permute-start.1
  353.8 33.6 %all_gather.20 = f32[1024,128]{1,0:T(8,128)S(1)} all-gather(f32[64,128]{1,0:T(8,128)S(1)} %fusion.31), channel_id=1, replica_groups=mesh['leaf'=32,'front'=16] {'front'}, dimensions={0}, use_global_device_ids=true | all-gather | bytes 557056 | tf_op jit(solution)/shard_map/all_gather | solution.py:60
  388.3 30.1 %all_gather.21 = f32[1024,128]{1,0:T(8,128)S(1)} all-gather(f32[64,128]{1,0:T(8,128)S(1)} %collective-permute-done.1), channel_id=1, replica_groups=mesh['leaf'=32,'front'=16] {'front'}, dimensions={0}, use_global_device_ids=true | all-gather | bytes 557056 | tf_op jit(solution)/shard_map/all_gather | solution.py:61
  421.3 126.1 %all-reduce.11.cloned.1.call-done = f32[2,2,64,128]{3,2,1,0:T(8,128)} async-done(((f32[2,2,64,128]{3,2,1,0:T(8,128)}), f32[2,2,64,128]{3,2,1,0:T(8,128)}) %all-reduce.11.cloned.1.call-update) | async-done | bytes 131088 | tf_op jit(solution)/shard_map/psum | solution.py:21
  548.2 5.2 collective-permute-start.2
  553.4 33.3 %all_gather.22 = f32[1024,128]{1,0:T(8,128)S(1)} all-gather(f32[64,128]{1,0:T(8,128)S(1)} %fusion.30), channel_id=1, replica_groups=mesh['leaf'=32,'front'=16] {'front'}, dimensions={0}, use_global_device_ids=true | all-gather | bytes 557056 | tf_op jit(solution)/shard_map/all_gather | solution.py:60
  587.6 30.3 %all_gather.23 = f32[1024,128]{1,0:T(8,128)S(1)} all-gather(f32[64,128]{1,0:T(8,128)S(1)} %collective-permute-done.2), channel_id=1, replica_groups=mesh['leaf'=32,'front'=16] {'front'}, dimensions={0}, use_global_device_ids=true | all-gather | bytes 557056 | tf_op jit(solution)/shard_map/all_gather | solution.py:61
  617.9 1.0 convolution_add_fusion
  620.7 120.9 %all-reduce.13.cloned.1.call-done = f32[1,2,64,128]{3,2,1,0:T(8,128)} async-done(((f32[1,2,64,128]{3,2,1,0:T(8,128)}), f32[1,2,64,128]{3,2,1,0:T(8,128)}) %all-reduce.13.cloned.1.call-update) | async-done | bytes 65552 | tf_op jit(solution)/shard_map/psum | solution.py:21
  742.6 56.8 %psum.60 = f32[32,128]{1,0:T(8,128)S(1)} all-reduce(f32[32,128]{1,0:T(8,128)S(1)} %convolution_bitcast_fusion.5), channel_id=1, replica_groups=mesh['leaf'=32,'front'=16] {'front'}, use_global_device_ids=true, to_apply=%region_4.5 | all-reduce | flops 4096 | bytes 32768 | tf_op jit(solution)/shard_map/psum | solution.py:126
  799.4 1.9 collective-permute-start.3
  801.3 1.1 collective-permute-done.3
  802.4 3.4 collective-permute-start.4
  805.8 2.4 collective-permute-done.4
  808.2 4.6 collective-permute-start.5
  812.8 3.1 collective-permute-done.5
  815.9 3.3 collective-permute-start.6
  819.3 3.5 collective-permute-done.6
  822.8 4.1 collective-permute-start.7
  827.6 4.9 collective-permute-done.7
  832.7 1.1 fusion.5
  834.2 53.5 %psum.61 = f32[64,128]{1,0:T(8,128)S(1)} all-reduce(f32[64,128]{1,0:T(8,128)S(1)} %convolution_bitcast_fusion.4), channel_id=1, replica_groups=mesh['leaf'=32,'front'=16] {'front'}, use_global_device_ids=true, to_apply=%region_5.6 | all-reduce | flops 8192 | bytes 65536 | tf_op jit(solution)/shard_map/psum | solution.py:126
  887.7 1.9 collective-permute-start.8
  889.6 1.2 collective-permute-done.8
  890.8 3.4 collective-permute-start.9
  894.1 2.8 collective-permute-done.9
  896.9 4.6 collective-permute-start.10
  901.5 3.8 collective-permute-done.10
  905.3 3.5 collective-permute-start.11
  909.8 3.8 collective-permute-done.11
  913.7 1.1 fusion.3
  915.9 129.0 %all-reduce.15.cloned.1.call-done = f32[128,128]{0,1:T(8,128)} async-done(((f32[128,128]{0,1:T(8,128)}), f32[128,128]{0,1:T(8,128)}) %all-reduce.15.cloned.1.call-update) | async-done | bytes 65552 | tf_op jit(solution)/shard_map/psum | solution.py:126
  1044.9 1.9 collective-permute-start.12
  1046.8 1.4 collective-permute-done.12
  1049.1 3.4 collective-permute-start.13
  1053.4 3.2 collective-permute-done.13
  1056.6 4.9 collective-permute-start.14
  1063.1 4.4 collective-permute-done.14
  1068.0 1.1 fusion.1
  1069.2 1.0 convolution_bitcast_fusion
  1071.7 128.7 %all-reduce.17.cloned.1.call-done = f32[256,128]{0,1:T(8,128)} async-done(((f32[256,128]{0,1:T(8,128)}), f32[256,128]{0,1:T(8,128)}) %all-reduce.17.cloned.1.call-update) | async-done | bytes 131088 | tf_op jit(solution)/shard_map/psum | solution.py:126
  (101 shorter events, 25.7 us)
Async XLA Ops:
  7.2 0.9 copy-start
  7.2 142.3 %all-reduce.7.cloned.1.call-start = ((), (), s32[]{:S(2)}) async-start(), calls=%async_computation | async-start | bytes 1048576 | tf_op jit(solution)/shard_map/psum | solution.py:21
  10.2 339.9 %all-reduce.9.cloned.1.call-start = ((), (), s32[]{:S(2)}) async-start(), calls=%async_computation.1 | async-start | bytes 524288 | tf_op jit(solution)/shard_map/psum | solution.py:21
  150.2 38.2 %collective-permute-start = (f32[64,128]{1,0:T(8,128)S(1)}, f32[64,128]{1,0:T(8,128)S(1)}, u32[]{:S(2)}, u32[]{:S(2)}) collective-permute-start(f32[64,128]{1,0:T(8,128)S(1)} %fusion.32), channel_id=1, source_target_pairs={{0,64},{16,80},{32,96},{48,112},{64,0},{80,16},{96,32},{112,48},{1... | collective-permute-start | bytes 98312 | tf_op jit(solution)/shard_map/ppermute | solution.py:12
  220.1 0.8 copy-start.3
  220.1 0.9 copy-start.7
  222.0 325.4 %all-reduce.11.cloned.1.call-start = ((), (), s32[]{:S(2)}) async-start(), calls=%async_computation.2 | async-start | bytes 262144 | tf_op jit(solution)/shard_map/psum | solution.py:21
  350.8 37.5 %collective-permute-start.1 = (f32[64,128]{1,0:T(8,128)S(1)}, f32[64,128]{1,0:T(8,128)S(1)}, u32[]{:S(2)}, u32[]{:S(2)}) collective-permute-start(f32[64,128]{1,0:T(8,128)S(1)} %fusion.31), channel_id=1, source_target_pairs={{0,128},{16,144},{32,160},{48,176},{64,192},{80,208},{96,224},{112... | collective-permute-start | bytes 98312 | tf_op jit(solution)/shard_map/ppermute | solution.py:12
  419.4 0.8 copy-start.2
  419.5 0.8 copy-start.8
  421.2 320.4 %all-reduce.13.cloned.1.call-start = ((), (), s32[]{:S(2)}) async-start(), calls=%async_computation.3 | async-start | bytes 131072 | tf_op jit(solution)/shard_map/psum | solution.py:21
  548.2 39.5 %collective-permute-start.2 = (f32[64,128]{1,0:T(8,128)S(1)}, f32[64,128]{1,0:T(8,128)S(1)}, u32[]{:S(2)}, u32[]{:S(2)}) collective-permute-start(f32[64,128]{1,0:T(8,128)S(1)} %fusion.30), channel_id=1, source_target_pairs={{0,256},{16,272},{32,288},{48,304},{64,320},{80,336},{96,352},{112... | collective-permute-start | bytes 98312 | tf_op jit(solution)/shard_map/ppermute | solution.py:12
  618.9 0.8 copy-start.5
  619.0 0.8 copy-start.9
  619.0 1.7 copy-start.1
  620.7 424.2 %all-reduce.15.cloned.1.call-start = ((), (), s32[]{:S(2)}) async-start(), calls=%async_computation.4 | async-start | bytes 131072 | tf_op jit(solution)/shard_map/psum | solution.py:126
  799.4 3.1 collective-permute-start.3
  802.4 5.8 collective-permute-start.4
  808.2 7.7 collective-permute-start.5
  815.9 6.9 collective-permute-start.6
  822.8 9.8 collective-permute-start.7
  887.7 3.1 collective-permute-start.8
  890.8 6.2 collective-permute-start.9
  896.9 8.4 collective-permute-start.10
  905.3 8.3 collective-permute-start.11
  915.9 284.5 %all-reduce.17.cloned.1.call-start = ((), (), s32[]{:S(2)}) async-start(), calls=%async_computation.5 | async-start | bytes 262144 | tf_op jit(solution)/shard_map/psum | solution.py:126
  1044.9 3.3 collective-permute-start.12
  1049.1 7.5 collective-permute-start.13
  1053.4 8.8 copy-start.6
  1056.6 10.9 collective-permute-start.14
  1070.1 0.8 copy-start.4
Sparse Core Ops, SparseCore 0:
  11.2 138.1 all-reduce.6
  222.1 127.8 all-reduce.8
  421.4 126.0 all-reduce.10
  620.8 120.7 all-reduce.12
  916.0 128.8 all-reduce.14
  1070.3 130.0 all-reduce.16
where the time goes:
time: 1210 us
  waiting for transfers between devices  806 us (67%)
  blocking collectives  301 us (25%)
  starting transfers between devices  53.6 us (4%)
  between operations  14.8 us (1%)
  matrix products  13.7 us (1%)
    psum x4, waiting for transfers between devices, group_total(): totals = lax.psum(spread_out, 'leaf')  513 us
    psum x2, waiting for transfers between devices, on_device(): column_block = lax.psum(partial_sum, 'front')  258 us
    psum x2, blocking collectives, on_device(): column_block = lax.psum(partial_sum, 'front')  110 us
    all_gather x3, blocking collectives, lift_update(): lax.all_gather(update_block, 'front', axis=0, tiled=True)  100 us
    all_gather x3, blocking collectives, lift_update(): lax.all_gather(partner_block, 'front', axis=0, tiled=True)  91 us
    ppermute x15, starting transfers between devices, partner_2(): return lax.ppermute(value, axis, pairs)  53.4 us
    ppermute x15, waiting for transfers between devices, partner_2(): return lax.ppermute(value, axis, pairs)  35.6 us
  transfers between devices with their start and end apart: 21, of which 18 were waited for; matrix products, arithmetic and copies ran while one was open for 1% of the time, Pallas kernels for 0%

commit v1 on v0

--- a/solution.py
+++ b/solution.py
@@ -4,6 +4,19 @@
 from jax.sharding import PartitionSpec as P
 
 exact_precision = lax.Precision.HIGHEST
+
+
+def ring_gather(array, axis, dim):
+    ways = lax.axis_size(axis)
+    up = [(d, (d + 1) % ways) for d in range(ways)]
+    down = [(d, (d - 1) % ways) for d in range(ways)]
+    earlier, later = ([array], [array])
+    for _ in range(ways // 2):
+        earlier.append(lax.ppermute(earlier[-1], axis, up))
+    for _ in range((ways - 1) // 2):
+        later.append(lax.ppermute(later[-1], axis, down))
+    line = jnp.concatenate([*earlier[::-1], *later[1:]], axis=dim)
+    return jnp.roll(line, (lax.axis_index(axis) - ways // 2) * array.shape[dim], axis=dim)
 
 
 def partner_2(value, axis, distance):
@@ -58,7 +71,7 @@
     partner_block = partner_2(update_block, "leaf", group_bits)
     own_full, other_full = (
         lax.all_gather(update_block, "front", axis=0, tiled=True),
-        lax.all_gather(partner_block, "front", axis=0, tiled=True),
+        ring_gather(partner_block, "front", 0),
     )
     placed = place_blocks(own_map, own_full, block_rows) + place_blocks(
         other_map, other_full, block_rows

time: 1210 us -> 1310 us (1.083)
  starting transfers between devices: 53.6 us -> 202 us
  blocking collectives: 301 us -> 210 us
  waiting for transfers between devices: 806 us -> 842 us
    ppermute x0 -> x45, starting transfers between devices: none -> 149 us  [the longest x21 92.1 us: ring_gather(): later.append(lax.ppermute(later[-1], axis, down))]
    all_gather x3 -> x0, blocking collectives: 91 us -> none  [lift_update(): lax.all_gather(partner_block, 'front', axis=0, tiled=True)]
    ppermute x0 -> x45, waiting for transfers between devices: none -> 20.6 us  [the longest x24 13.2 us: ring_gather(): earlier.append(lax.ppermute(earlier[-1], axis, up))]
  transfers between devices with their start and end apart: 21 -> 66, of which waited for: 18 -> 27; matrix products, arithmetic and copies ran while one was open for 1% -> 1% of each run, Pallas kernels for 0% -> 0%
where the time goes in v1:
time: 1310 us; the launch traced here: 1300 us
  waiting for transfers between devices  842 us (64%)
  blocking collectives  210 us (16%)
  starting transfers between devices  202 us (15%)
  between operations  15.8 us (1%)
  matrix products  13.7 us (1%)
    psum x4, waiting for transfers between devices, group_total(): totals = lax.psum(spread_out, 'leaf')  520 us
    psum x2, waiting for transfers between devices, on_device(): column_block = lax.psum(partial_sum, 'front')  258 us
    psum x2, blocking collectives, on_device(): column_block = lax.psum(partial_sum, 'front')  110 us
    all_gather x3, blocking collectives, lift_update(): lax.all_gather(update_block, 'front', axis=0, tiled=True)  100 us
    ppermute x21, starting transfers between devices, ring_gather(): later.append(lax.ppermute(later[-1], axis, down))  92.1 us
    ppermute x24, starting transfers between devices, ring_gather(): earlier.append(lax.ppermute(earlier[-1], axis, up))  56.6 us
    ppermute x15, starting transfers between devices, partner_2(): return lax.ppermute(value, axis, pairs)  53.2 us
    ppermute x15, waiting for transfers between devices, partner_2(): return lax.ppermute(value, axis, pairs)  43.7 us
  transfers between devices with their start and end apart: 66, of which 27 were waited for; matrix products, arithmetic and copies ran while one was open for 1% of the time, Pallas kernels for 0%

profile of v1, /device:TPU:2, one launch (start us, length us, event | category | flops | bytes accessed | tf_op | source)
XLA Modules:
  0.0 1304.5 jit_solution(1061403018717849188)
XLA Ops:
  10.2 139.2 %all-reduce.7.cloned.1.call-done = f32[8,2,64,128]{3,2,1,0:T(8,128)} async-done(((f32[8,2,64,128]{3,2,1,0:T(8,128)}), f32[8,2,64,128]{3,2,1,0:T(8,128)}) %all-reduce.7.cloned.1.call-update) | async-done | bytes 524304 | tf_op jit(solution)/shard_map/psum | solution.py:34
  150.2 4.2 collective-permute-start
  157.5 3.5 collective-permute-start.1
  161.0 4.4 collective-permute-done.1
  167.3 5.1 collective-permute-start.9
  174.4 5.1 collective-permute-start.10
  181.5 5.1 collective-permute-start.11
  189.4 5.1 collective-permute-start.12
  196.6 5.1 collective-permute-start.13
  203.6 33.5 %all_gather.9 = f32[1024,128]{1,0:T(8,128)S(1)} all-gather(f32[64,128]{1,0:T(8,128)S(1)} %fusion.35), channel_id=1, replica_groups=mesh['leaf'=32,'front'=16] {'front'}, dimensions={0}, use_global_device_ids=true | all-gather | bytes 557056 | tf_op jit(solution)/shard_map/all_gather | solution.py:73
  239.1 3.9 collective-permute-start.8
  253.1 129.4 %all-reduce.9.cloned.1.call-done = f32[4,2,64,128]{3,2,1,0:T(8,128)} async-done(((f32[4,2,64,128]{3,2,1,0:T(8,128)}), f32[4,2,64,128]{3,2,1,0:T(8,128)}) %all-reduce.9.cloned.1.call-update) | async-done | bytes 262160 | tf_op jit(solution)/shard_map/psum | solution.py:34
  389.0 3.4 collective-permute-start.17
  392.5 4.4 collective-permute-done.17
  398.8 5.1 collective-permute-start.25
  405.9 5.1 collective-permute-start.26
  413.0 5.1 collective-permute-start.27
  420.1 5.1 collective-permute-start.28
  427.2 5.1 collective-permute-start.29
  434.3 33.2 %all_gather.10 = f32[1024,128]{1,0:T(8,128)S(1)} all-gather(f32[64,128]{1,0:T(8,128)S(1)} %fusion.34), channel_id=1, replica_groups=mesh['leaf'=32,'front'=16] {'front'}, dimensions={0}, use_global_device_ids=true | all-gather | bytes 557056 | tf_op jit(solution)/shard_map/all_gather | solution.py:73
  469.4 3.9 collective-permute-start.24
  483.3 128.1 %all-reduce.11.cloned.1.call-done = f32[2,2,64,128]{3,2,1,0:T(8,128)} async-done(((f32[2,2,64,128]{3,2,1,0:T(8,128)}), f32[2,2,64,128]{3,2,1,0:T(8,128)}) %all-reduce.11.cloned.1.call-update) | async-done | bytes 131088 | tf_op jit(solution)/shard_map/psum | solution.py:34
  612.2 5.2 collective-permute-start.32
  619.5 3.5 collective-permute-start.33
  622.9 4.4 collective-permute-done.33
  629.2 5.1 collective-permute-start.41
  636.3 5.1 collective-permute-start.42
  643.4 5.1 collective-permute-start.43
  650.5 5.1 collective-permute-start.44
  657.6 5.1 collective-permute-start.45
  664.7 33.2 %all_gather.11 = f32[1024,128]{1,0:T(8,128)S(1)} all-gather(f32[64,128]{1,0:T(8,128)S(1)} %fusion.33), channel_id=1, replica_groups=mesh['leaf'=32,'front'=16] {'front'}, dimensions={0}, use_global_device_ids=true | all-gather | bytes 557056 | tf_op jit(solution)/shard_map/all_gather | solution.py:73
  699.8 3.9 collective-permute-start.40
  713.8 123.5 %all-reduce.13.cloned.1.call-done = f32[1,2,64,128]{3,2,1,0:T(8,128)} async-done(((f32[1,2,64,128]{3,2,1,0:T(8,128)}), f32[1,2,64,128]{3,2,1,0:T(8,128)}) %all-reduce.13.cloned.1.call-update) | async-done | bytes 65552 | tf_op jit(solution)/shard_map/psum | solution.py:34
  838.3 56.8 %psum.60 = f32[32,128]{1,0:T(8,128)S(1)} all-reduce(f32[32,128]{1,0:T(8,128)S(1)} %convolution_bitcast_fusion.5), channel_id=1, replica_groups=mesh['leaf'=32,'front'=16] {'front'}, use_global_device_ids=true, to_apply=%region_4.6 | all-reduce | flops 4096 | bytes 32768 | tf_op jit(solution)/shard_map/psum | solution.py:139
  898.1 3.4 collective-permute-start.49
  903.9 4.6 collective-permute-start.50
  914.9 3.5 collective-permute-done.51
  918.5 4.1 collective-permute-start.52
  923.3 4.9 collective-permute-done.52
  929.8 53.5 %psum.61 = f32[64,128]{1,0:T(8,128)S(1)} all-reduce(f32[64,128]{1,0:T(8,128)S(1)} %convolution_bitcast_fusion.4), channel_id=1, replica_groups=mesh['leaf'=32,'front'=16] {'front'}, use_global_device_ids=true, to_apply=%region_5.7 | all-reduce | flops 8192 | bytes 65536 | tf_op jit(solution)/shard_map/psum | solution.py:139
  992.6 4.6 collective-permute-start.55
  997.2 3.8 collective-permute-done.55
  1005.3 4.0 collective-permute-done.56
  1011.6 129.0 %all-reduce.15.cloned.1.call-done = f32[128,128]{0,1:T(8,128)} async-done(((f32[128,128]{0,1:T(8,128)}), f32[128,128]{0,1:T(8,128)}) %all-reduce.15.cloned.1.call-update) | async-done | bytes 65552 | tf_op jit(solution)/shard_map/psum | solution.py:139
  1144.8 3.4 collective-permute-start.58
  1152.3 4.9 collective-permute-start.59
  1158.8 4.4 collective-permute-done.59
  1167.4 128.6 %all-reduce.17.cloned.1.call-done = f32[256,128]{0,1:T(8,128)} async-done(((f32[256,128]{0,1:T(8,128)}), f32[256,128]{0,1:T(8,128)}) %all-reduce.17.cloned.1.call-update) | async-done | bytes 131088 | tf_op jit(solution)/shard_map/psum | solution.py:139
  (239 shorter events, 133.5 us)
Async XLA Ops:
  7.2 142.3 %all-reduce.7.cloned.1.call-start = ((), (), s32[]{:S(2)}) async-start(), calls=%async_computation | async-start | bytes 1048576 | tf_op jit(solution)/shard_map/psum | solution.py:34
  10.2 372.3 %all-reduce.9.cloned.1.call-start = ((), (), s32[]{:S(2)}) async-start(), calls=%async_computation.1 | async-start | bytes 524288 | tf_op jit(solution)/shard_map/psum | solution.py:34
  150.2 7.3 collective-permute-start
  157.5 7.8 collective-permute-start.1
  167.3 7.1 collective-permute-start.9
  172.4 7.1 collective-permute-start.3
  174.4 7.1 collective-permute-start.10
  179.5 7.1 collective-permute-start.4
  181.5 7.9 collective-permute-start.11
  186.6 7.9 collective-permute-start.5
  189.4 7.1 collective-permute-start.12
  194.6 7.1 collective-permute-start.6
  196.6 40.6 %collective-permute-start.13 = (f32[64,128]{1,0:T(8,128)S(1)}, f32[64,128]{1,0:T(8,128)S(1)}, u32[]{:S(2)}, u32[]{:S(2)}) collective-permute-start(f32[64,128]{1,0:T(8,128)S(1)} %collective-permute-done.12), channel_id=1, source_target_pairs={{0,15},{1,0},{2,1},{3,2},{4,3},{5,4},{6,5},{7,6},{8,7},{9,8},{10,9... | collective-permute-start | bytes 98312 | tf_op jit(solution)/shard_map/ppermute | solution.py:17
  201.7 37.4 %collective-permute-start.7 = (f32[64,128]{1,0:T(8,128)S(1)}, f32[64,128]{1,0:T(8,128)S(1)}, u32[]{:S(2)}, u32[]{:S(2)}) collective-permute-start(f32[64,128]{1,0:T(8,128)S(1)} %collective-permute-done.6), channel_id=1, source_target_pairs={{0,1},{1,2},{2,3},{3,4},{4,5},{5,6},{6,7},{7,8},{8,9},{9,10},{10,1... | collective-permute-start | bytes 98312 | tf_op jit(solution)/shard_map/ppermute | solution.py:15
  239.1 8.0 collective-permute-start.8
  253.0 358.4 %all-reduce.11.cloned.1.call-start = ((), (), s32[]{:S(2)}) async-start(), calls=%async_computation.2 | async-start | bytes 262144 | tf_op jit(solution)/shard_map/psum | solution.py:34
  389.0 7.8 collective-permute-start.17
  398.8 7.1 collective-permute-start.25
  403.9 7.1 collective-permute-start.19
  405.9 7.1 collective-permute-start.26
  411.0 7.1 collective-permute-start.20
  413.0 7.1 collective-permute-start.27
  418.1 7.1 collective-permute-start.21
  420.1 7.1 collective-permute-start.28
  425.2 7.1 collective-permute-start.22
  427.2 40.3 %collective-permute-start.29 = (f32[64,128]{1,0:T(8,128)S(1)}, f32[64,128]{1,0:T(8,128)S(1)}, u32[]{:S(2)}, u32[]{:S(2)}) collective-permute-start(f32[64,128]{1,0:T(8,128)S(1)} %collective-permute-done.28), channel_id=1, source_target_pairs={{0,15},{1,0},{2,1},{3,2},{4,3},{5,4},{6,5},{7,6},{8,7},{9,8},{10,9... | collective-permute-start | bytes 98312 | tf_op jit(solution)/shard_map/ppermute | solution.py:17
  432.3 37.1 %collective-permute-start.23 = (f32[64,128]{1,0:T(8,128)S(1)}, f32[64,128]{1,0:T(8,128)S(1)}, u32[]{:S(2)}, u32[]{:S(2)}) collective-permute-start(f32[64,128]{1,0:T(8,128)S(1)} %collective-permute-done.22), channel_id=1, source_target_pairs={{0,1},{1,2},{2,3},{3,4},{4,5},{5,6},{6,7},{7,8},{8,9},{9,10},{10,1... | collective-permute-start | bytes 98312 | tf_op jit(solution)/shard_map/ppermute | solution.py:15
  469.4 8.0 collective-permute-start.24
  483.2 354.1 %all-reduce.13.cloned.1.call-start = ((), (), s32[]{:S(2)}) async-start(), calls=%async_computation.3 | async-start | bytes 131072 | tf_op jit(solution)/shard_map/psum | solution.py:34
  612.2 7.3 collective-permute-start.32
  619.5 7.8 collective-permute-start.33
  629.2 7.1 collective-permute-start.41
  634.4 7.1 collective-permute-start.35
  636.3 7.1 collective-permute-start.42
  641.5 7.1 collective-permute-start.36
  650.5 7.1 collective-permute-start.44
  655.6 7.1 collective-permute-start.38
  657.6 40.3 %collective-permute-start.45 = (f32[64,128]{1,0:T(8,128)S(1)}, f32[64,128]{1,0:T(8,128)S(1)}, u32[]{:S(2)}, u32[]{:S(2)}) collective-permute-start(f32[64,128]{1,0:T(8,128)S(1)} %collective-permute-done.44), channel_id=1, source_target_pairs={{0,15},{1,0},{2,1},{3,2},{4,3},{5,4},{6,5},{7,6},{8,7},{9,8},{10,9... | collective-permute-start | bytes 98312 | tf_op jit(solution)/shard_map/ppermute | solution.py:17
  662.8 37.1 %collective-permute-start.39 = (f32[64,128]{1,0:T(8,128)S(1)}, f32[64,128]{1,0:T(8,128)S(1)}, u32[]{:S(2)}, u32[]{:S(2)}) collective-permute-start(f32[64,128]{1,0:T(8,128)S(1)} %collective-permute-done.38), channel_id=1, source_target_pairs={{0,1},{1,2},{2,3},{3,4},{4,5},{5,6},{6,7},{7,8},{8,9},{9,10},{10,1... | collective-permute-start | bytes 98312 | tf_op jit(solution)/shard_map/ppermute | solution.py:15
  699.8 8.0 collective-permute-start.40
  713.5 427.0 %all-reduce.15.cloned.1.call-start = ((), (), s32[]{:S(2)}) async-start(), calls=%async_computation.4 | async-start | bytes 131072 | tf_op jit(solution)/shard_map/psum | solution.py:139
  903.9 7.7 collective-permute-start.50
  918.5 9.8 collective-permute-start.52
  992.6 8.4 collective-permute-start.55
  1001.0 8.3 collective-permute-start.56
  1011.5 284.5 %all-reduce.17.cloned.1.call-start = ((), (), s32[]{:S(2)}) async-start(), calls=%async_computation.5 | async-start | bytes 262144 | tf_op jit(solution)/shard_map/psum | solution.py:139
  1144.8 7.5 collective-permute-start.58
  1152.3 10.9 collective-permute-start.59
  (28 other events, 124.5 us)
Sparse Core Ops, SparseCore 0:
  11.2 138.1 all-reduce.6
  253.1 129.3 all-reduce.8
  483.3 128.0 all-reduce.10
  713.6 123.5 all-reduce.12
  1011.6 128.8 all-reduce.14
  1166.0 130.0 all-reduce.16
